TPU v7x, 32 devices: a whole 2x2x4 slice. The times are simulated.
32 devices in a mesh: region: 2 (over y), tile: 4 (over z), sub: 2 (over x), lane: 2 (over core).
Axes of the slice: x: 2, y: 2, z: 4, core: 2. Of those that a mesh axis runs over, the one named last changes fastest.
Arguments:
- state: float32 [3, 64, 128, 128], P(None, ('region', 'tile', 'sub', 'lane')), parts along dimension 1, may hold values from -5.04 to 5.04, as said below
- terrain_local: bfloat16 [2, 64, 128, 128], P(None, ('region', 'tile', 'sub', 'lane')), parts along dimension 1, may hold values from -0.9 to 0.9, as said below
- terrain_store: bfloat16 [2, 128, 128, 128], P(None, ('region', 'tile', 'sub', 'lane')), parts along dimension 1, may hold values from -0.9 to 0.9, as said below
- wet_count: int32 [32], P(('region', 'tile', 'sub', 'lane')), parts along dimension 0, may hold values from 1 to 2, as said below
- face_links: int32 [64, 2, 4], P(('region', 'tile', 'sub', 'lane')), parts along dimension 0, may hold values from -1 to 15, as said below
- new_source: int32 [64], P(('region', 'tile', 'sub', 'lane')), parts along dimension 0, may hold values from -1 to 3, as said below
- store_target: int32 [128], P(('region', 'tile', 'sub', 'lane')), parts along dimension 0, may hold values from -1 to 3, as said below
Outputs:
- state_out: float32 [3, 64, 128, 128], P(None, ('region', 'tile', 'sub', 'lane')), parts along dimension 1
There are 2 independent parts, one for each index of `region`. A program takes and returns all parts, laid end to end along the dimension named above; each array names one. Nothing has to cross between parts.
Inputs may be any that keep to these rules, and one draw needn't show every extreme that they name: state[0] is a water depth of 0.7 to 4.2; the discharges state[1] and state[2] are at most 1.2 times the depth in magnitude. terrain_local[0] is a bed elevation, terrain_local[1] a Manning coefficient of 0.03 to 0.3. terrain_store[0] is a bed elevation, terrain_store[1] a Manning coefficient of 0.03 to 0.3. A device's live tiles fill its first wet_count slots, the other slots are padding; some device has 2. `face_links`: [i, 0, f] is the device and [i, 1, f] the slot of the live tile across face f of tile i, both -1 where the face is a wall or i is padding; links are mutual (west with east, north with south); across west or east faces the device has the same tile index, across a north face a tile index one lower, across a south face one higher; the tiles of one device have at most 1 face of one direction linked to tiles of any one device, and some device has that many. `new_source`: -1 for live tiles that were wet before and for padding; for a newly wetted tile the tile index of the device that stores its terrain, which has the same sub and lane indices; no two new tiles of one device come from the same device; a device has at most 2 new tiles, and some device has that many. `store_target`: for each stored block, the tile index of the device (same sub and lane) whose new tile asks for it, or -1; every request of new_source names exactly one block of the storing device.
All inputs are finite; a program needn't handle non-finite values.
Results may differ from a plain program's by a relative error of at most 0.0004.
Values may be sent and summed in bfloat16 or wider, within the bound.
A program may use at most 64 MiB of HBM per device.

v0:
```python
import jax
import jax.numpy as jnp
from jax import lax
from jax.sharding import PartitionSpec as P

STEPS = 3


gravity_accel = 9.81
cell_width = 30.0
time_step = 1.0
mirror_signs = (
    (1.0, -1.0, 1.0, 1.0),
    (1.0, -1.0, 1.0, 1.0),
    (1.0, 1.0, -1.0, 1.0),
    (1.0, 1.0, -1.0, 1.0),
)


def from_behind(array, axis, by):
    peers = lax.axis_size(axis)
    pairs = [(i, i + by) for i in range(peers) if 0 <= i + by < peers]
    return lax.ppermute(array, axis, pairs)


def face_flux(
    depth_left,
    normal_left,
    tangent_left,
    level_left,
    depth_right,
    normal_right,
    tangent_right,
    level_right,
):
    level_face = jnp.maximum(level_left, level_right)
    held_left = jnp.maximum(depth_left + level_left - level_face, 0.0)
    held_right = jnp.maximum(depth_right + level_right - level_face, 0.0)
    speed_left = normal_left / depth_left
    speed_right = normal_right / depth_right
    drift_left = tangent_left / depth_left
    drift_right = tangent_right / depth_right
    wave_speed = jnp.maximum(
        jnp.abs(speed_left) + jnp.sqrt(gravity_accel * held_left),
        jnp.abs(speed_right) + jnp.sqrt(gravity_accel * held_right),
    )
    push_left = held_left * speed_left * speed_left + 0.5 * gravity_accel * held_left * held_left
    push_right = (
        held_right * speed_right * speed_right + 0.5 * gravity_accel * held_right * held_right
    )
    mass_flux = 0.5 * (held_left * speed_left + held_right * speed_right) - 0.5 * wave_speed * (
        held_right - held_left
    )
    normal_flux = 0.5 * (push_left + push_right) - 0.5 * wave_speed * (
        held_right * speed_right - held_left * speed_left
    )
    tangent_flux = 0.5 * (
        held_left * speed_left * drift_left + held_right * speed_right * drift_right
    ) - 0.5 * wave_speed * (held_right * drift_right - held_left * drift_left)
    source_left = 0.5 * gravity_accel * (depth_left * depth_left - held_left * held_left)
    source_right = 0.5 * gravity_accel * (depth_right * depth_right - held_right * held_right)
    return (mass_flux, normal_flux, tangent_flux, source_left, source_right)


def advance(fields, roughness, ghosts):
    west_side, east_side, north_side, south_side = (ghosts[0], ghosts[1], ghosts[2], ghosts[3])

    def across(field_index):
        return jnp.concatenate(
            [
                west_side[field_index][:, :, None],
                fields[field_index],
                east_side[field_index][:, :, None],
            ],
            axis=2,
        )

    def upward(field_index):
        return jnp.concatenate(
            [
                north_side[field_index][:, None, :],
                fields[field_index],
                south_side[field_index][:, None, :],
            ],
            axis=1,
        )

    depth_x, along_x, cross_x, level_x = (across(0), across(1), across(2), across(3))
    east_terms = face_flux(
        depth_x[:, :, :-1],
        along_x[:, :, :-1],
        cross_x[:, :, :-1],
        level_x[:, :, :-1],
        depth_x[:, :, 1:],
        along_x[:, :, 1:],
        cross_x[:, :, 1:],
        level_x[:, :, 1:],
    )
    depth_y, along_y, cross_y, level_y = (upward(0), upward(1), upward(2), upward(3))
    north_terms = face_flux(
        depth_y[:, :-1],
        cross_y[:, :-1],
        along_y[:, :-1],
        level_y[:, :-1],
        depth_y[:, 1:],
        cross_y[:, 1:],
        along_y[:, 1:],
        level_y[:, 1:],
    )
    change_depth = (
        east_terms[0][:, :, 1:]
        - east_terms[0][:, :, :-1]
        + (north_terms[0][:, 1:] - north_terms[0][:, :-1])
    )
    change_along = (
        east_terms[1][:, :, 1:]
        + east_terms[3][:, :, 1:]
        - (east_terms[1][:, :, :-1] + east_terms[4][:, :, :-1])
        + (north_terms[2][:, 1:] - north_terms[2][:, :-1])
    )
    change_cross = (
        east_terms[2][:, :, 1:]
        - east_terms[2][:, :, :-1]
        + (
            north_terms[1][:, 1:]
            + north_terms[3][:, 1:]
            - (north_terms[1][:, :-1] + north_terms[4][:, :-1])
        )
    )
    step_ratio = time_step / cell_width
    depth_new = fields[0] - step_ratio * change_depth
    along_new = fields[1] - step_ratio * change_along
    cross_new = fields[2] - step_ratio * change_cross
    flow_speed = jnp.sqrt(along_new * along_new + cross_new * cross_new) / depth_new
    damping = 1.0 + time_step * gravity_accel * roughness * roughness * flow_speed / jnp.power(
        depth_new, 4.0 / 3.0
    )
    return (depth_new, along_new / damping, cross_new / damping)


def face_strips(fields):
    return jnp.stack(
        [fields[:, :, :, 0], fields[:, :, :, -1], fields[:, :, 0, :], fields[:, :, -1, :]]
    )


def unpack_band(arrived, link_device, link_slot, peer_count):
    slot_count = link_device.shape[0]
    linked = link_device >= 0
    position = link_device % peer_count * slot_count + link_slot
    select = (
        (position[:, None] == jnp.arange(peer_count * slot_count)[None, :]) & linked[:, None]
    ).astype(jnp.float32)
    return jnp.einsum("kn,fnx->fkx", select, arrived, precision=lax.Precision.HIGHEST)


def route_faces(strips, link_device, link_slot, peer_count):
    outgoing = [strips[face_index] for face_index in range(4)]
    from_north = from_behind(outgoing[3], "tile", 1)
    from_south = from_behind(outgoing[2], "tile", -1)
    pooled = jnp.stack([outgoing[1], outgoing[0], from_north, from_south])
    arrived = lax.all_gather(pooled, ("sub", "lane"), axis=2, tiled=True)
    remote = [
        unpack_band(
            arrived[face_index], link_device[:, face_index], link_slot[:, face_index], peer_count
        )
        for face_index in range(4)
    ]
    return remote


def local(state, terrain_local, terrain_store, wet_count, face_links, new_source, store_target):
    slot_count = state.shape[1]
    band_count = lax.axis_size("tile")
    peer_count = lax.axis_size(("sub", "lane"))
    band_ids = jnp.arange(band_count, dtype=jnp.int32)
    sending = (store_target[None, :] == band_ids[:, None]).astype(jnp.bfloat16)
    outbound = jnp.einsum(
        "rj,cjxy->crxy", sending, terrain_store, preferred_element_type=jnp.float32
    ).astype(jnp.bfloat16)
    inbound = lax.all_to_all(outbound, "tile", split_axis=1, concat_axis=1, tiled=True)
    taking = (new_source[:, None] == band_ids[None, :]).astype(jnp.bfloat16)
    fetched = jnp.einsum("kq,cqxy->ckxy", taking, inbound, preferred_element_type=jnp.float32)
    terrain = jnp.where(
        (new_source >= 0)[None, :, None, None], fetched, terrain_local.astype(jnp.float32)
    )
    bed_level = terrain[0]
    roughness = terrain[1]
    link_device = face_links[:, 0, :]
    link_slot = face_links[:, 1, :]
    linked = link_device >= 0
    live_slot = jnp.arange(slot_count) < wet_count[0]
    depth_now, flow_x, flow_y = (state[0], state[1], state[2])
    bed_remote = route_faces(face_strips(bed_level[None]), link_device, link_slot, peer_count)
    for step_index in range(STEPS):
        fields = jnp.stack([depth_now, flow_x, flow_y, bed_level])
        moving = route_faces(face_strips(fields[:3]), link_device, link_slot, peer_count)
        remote = [
            jnp.concatenate([moving[face_index], bed_remote[face_index]], axis=0)
            for face_index in range(4)
        ]
        own_strips = face_strips(fields)
        ghosts = jnp.stack(
            [
                jnp.where(
                    linked[:, face_index][None, :, None],
                    remote[face_index],
                    own_strips[face_index]
                    * jnp.asarray(mirror_signs[face_index], jnp.float32)[:, None, None],
                )
                for face_index in range(4)
            ]
        )
        depth_now, flow_x, flow_y = advance(fields, roughness, ghosts)
    result = jnp.stack([depth_now, flow_x, flow_y])
    return jnp.where(live_slot[None, :, None, None], result, 0.0)


def solution(mesh):
    in_specs = (
        P(None, ("region", "tile", "sub", "lane"), None, None),
        P(None, ("region", "tile", "sub", "lane"), None, None),
        P(None, ("region", "tile", "sub", "lane"), None, None),
        P(("region", "tile", "sub", "lane")),
        P(("region", "tile", "sub", "lane"), None, None),
        P(("region", "tile", "sub", "lane")),
        P(("region", "tile", "sub", "lane")),
    )
    out_specs = P(None, ("region", "tile", "sub", "lane"), None, None)
    return jax.shard_map(local, mesh=mesh, in_specs=in_specs, out_specs=out_specs, check_vma=False)
```

profile of v0, /device:TPU:0, one launch (start us, length us, event | category | flops | bytes accessed | tf_op | source)
XLA Modules:
  0.0 102.6 jit_solution(7713131735411747922)
XLA Ops:
  2.1 5.6 %collective-permute-start = (f32[3,2,128]{2,1,0:T(2,128)S(1)}, f32[3,2,128]{2,1,0:T(2,128)S(1)}, u32[]{:S(2)}, u32[]{:S(2)}) collective-permute-start(f32[3,2,128]{2,1,0:T(2,128)S(1)} %bitcast.396), channel_id=1, source_target_pairs={{0,4},{4,8},{8,12},{1,5},{5,9},{9,13},{2,6},{6,10},{10,14},{3,7},{... | collective-permute-start | bytes 9224 | tf_op jit(solution)/shard_map/ppermute | solution.py:23
  8.7 4.4 %all-to-all-start = ((bf16[2,4,128,128]{3,2,0,1:T(8,128)(2,1)}), bf16[2,4,128,128]{3,2,0,1:T(8,128)(2,1)S(1)}, u32[]{:S(2)}, u32[]{:S(2)}) async-start(bf16[2,4,128,128]{3,2,0,1:T(8,128)(2,1)} %copy.2654), calls=%async_computation | async-start | bytes 524288 | tf_op jit(solution)/shard_map/all_to_all | solution.py:181
  16.2 5.2 %all_gather.12 = f32[4,3,8,128]{3,0,1,2:T(4,128)S(1)} all-gather(f32[4,3,2,128]{3,0,1,2:T(4,128)S(1)} %copy.2651), channel_id=1, replica_groups=mesh['region'=2,'tile'=4,'sub'=2,'lane'=2] {'sub','lane'}, dimensions={2}, use_global_device_ids=true | all-gather | bytes 61440 | tf_op jit(solution)/shard_map/all_gather | solution.py:162
  23.1 1.3 %collective-permute-start.3 = (f32[1,2,128]{2,1,0:T(2,128)S(1)}, f32[1,2,128]{2,1,0:T(2,128)S(1)}, u32[]{:S(2)}, u32[]{:S(2)}) collective-permute-start(f32[1,2,128]{2,1,0:T(2,128)S(1)} %bitcast.399), channel_id=1, source_target_pairs={{4,0},{8,4},{12,8},{5,1},{9,5},{13,9},{6,2},{10,6},{14,10},{7,3},{... | collective-permute-start | bytes 3080 | tf_op jit(solution)/shard_map/ppermute | solution.py:23
  24.4 4.5 %collective-permute-start.2 = (f32[1,2,128]{2,1,0:T(2,128)S(1)}, f32[1,2,128]{2,1,0:T(2,128)S(1)}, u32[]{:S(2)}, u32[]{:S(2)}) collective-permute-start(f32[1,2,128]{2,1,0:T(2,128)S(1)} %bitcast.398), channel_id=1, source_target_pairs={{0,4},{4,8},{8,12},{1,5},{5,9},{9,13},{2,6},{6,10},{10,14},{3,7},{... | collective-permute-start | bytes 3080 | tf_op jit(solution)/shard_map/ppermute | solution.py:23
  30.2 5.3 %all_gather.13 = f32[4,1,8,128]{3,0,1,2:T(4,128)S(1)} all-gather(f32[4,1,2,128]{3,0,1,2:T(4,128)S(1)} %copy.2659), channel_id=1, replica_groups=mesh['region'=2,'tile'=4,'sub'=2,'lane'=2] {'sub','lane'}, dimensions={2}, use_global_device_ids=true | all-gather | bytes 20480 | tf_op jit(solution)/shard_map/all_gather | solution.py:162
  38.9 2.3 %fusion.9 = (f32[2,128,129]{2,0,1:T(2,128)S(1)}, f32[2,128,129]{2,0,1:T(2,128)S(1)}, f32[2,128,129]{2,0,1:T(2,128)S(1)}) fusion(f32[2,128,1]{2,0,1:T(2,128)S(1)} %copy.2672, f32[2,128,128]{2,0,1:T(2,128)S(1)} %bitcast.348, f32[2,128,1]{2,0,1:T(2,128)S(1)} %copy.2674, f32[2,128,128]{2,0,1:T(2,128)S(1)} %get-tuple-element.172, f32[2,128,1]{2,0,1:T(2,128)S(1)} %copy.2661, ...), kind=kLoop, calls=%fused_computation.70 | loop fusion | flops 1254912 | bytes 795648 | tf_op jit(solution)/shard_map/sub | solution.py:54
  41.2 1.7 %fusion.27 = f32[2,128,129]{2,0,1:T(2,128)S(1)} fusion(f32[2,128,129]{2,0,1:T(2,128)S(1)} %get-tuple-element.50, f32[2,128,129]{2,0,1:T(2,128)S(1)} %get-tuple-element.51, f32[2,128,1]{2,0,1:T(2,128)S(1)} %copy.2672, f32[2,128,128]{2,0,1:T(2,128)S(1)} %bitcast.349, f32[2,128,1]{2,0,1:T(2,128)S(1)} %copy.2674, f32[2,128,128]{2,0,1:T(2,128)S(1)} %get-tuple-element.172, ...), kind=kLoop, calls=%fused_computation.112 | loop fusion | flops 693504 | bytes 662528 | tf_op jit(solution)/shard_map/sub | solution.py:51
  42.9 2.1 %multiply_subtract_fusion.2 = f32[2,128,129]{2,0,1:T(2,128)S(1)} fusion(f32[2,128,129]{2,0,1:T(2,128)S(1)} %get-tuple-element.51, f32[2,128,129]{2,0,1:T(2,128)S(1)} %get-tuple-element.50, f32[2,128,1]{2,0,1:T(2,128)S(1)} %copy.2694, f32[2,128,128]{2,0,1:T(2,128)S(1)} %get-tuple-element.171, f32[2,128,1]{2,0,1:T(2,128)S(1)} %copy.2691, ...), kind=kLoop, calls=%fused_computation.109 | loop fusion | flops 957696 | bytes 795648 | tf_op jit(solution)/shard_map/sub | solution.py:57
  46.5 2.1 %fusion.200 = (f32[2,128,128]{2,0,1:T(2,128)S(1)}, f32[2,128,128]{2,0,1:T(2,128)S(1)}, f32[2,128,128]{2,0,1:T(2,128)S(1)}, f32[2,128,128]{2,0,1:T(2,128)S(1)}) fusion(f32[2,128,128]{2,0,1:T(2,128)S(1)} %copy.2689, f32[2,129,128]{2,0,1:T(2,128)S(1)} %get-tuple-element.62, f32[2,128,129]{2,0,1:T(2,128)S(1)} %fusion.27, ...), kind=kLoop, calls=%fused_computation.486 | loop fusion | flops 1605632 | bytes 3280896 | tf_op jit(solution)/shard_map/div | solution.py:138
  50.3 1.3 %collective-permute-start.5 = (f32[3,2,128]{2,1,0:T(2,128)S(1)}, f32[3,2,128]{2,1,0:T(2,128)S(1)}, u32[]{:S(2)}, u32[]{:S(2)}) collective-permute-start(f32[3,2,128]{2,1,0:T(2,128)S(1)} %bitcast.388), channel_id=1, source_target_pairs={{4,0},{8,4},{12,8},{5,1},{9,5},{13,9},{6,2},{10,6},{14,10},{7,3},{... | collective-permute-start | bytes 9224 | tf_op jit(solution)/shard_map/ppermute | solution.py:23
  51.6 4.8 %collective-permute-start.4 = (f32[3,2,128]{2,1,0:T(2,128)S(1)}, f32[3,2,128]{2,1,0:T(2,128)S(1)}, u32[]{:S(2)}, u32[]{:S(2)}) collective-permute-start(f32[3,2,128]{2,1,0:T(2,128)S(1)} %bitcast.386), channel_id=1, source_target_pairs={{0,4},{4,8},{8,12},{1,5},{5,9},{9,13},{2,6},{6,10},{10,14},{3,7},{... | collective-permute-start | bytes 9224 | tf_op jit(solution)/shard_map/ppermute | solution.py:23
  57.7 5.5 %all_gather.14 = f32[4,3,8,128]{3,0,1,2:T(4,128)S(1)} all-gather(f32[4,3,2,128]{3,0,1,2:T(4,128)S(1)} %copy.2700), channel_id=1, replica_groups=mesh['region'=2,'tile'=4,'sub'=2,'lane'=2] {'sub','lane'}, dimensions={2}, use_global_device_ids=true | all-gather | bytes 61440 | tf_op jit(solution)/shard_map/all_gather | solution.py:162
  65.2 2.3 %fusion.14 = (f32[2,128,129]{2,0,1:T(2,128)S(1)}, f32[2,128,129]{2,0,1:T(2,128)S(1)}, f32[2,128,129]{2,0,1:T(2,128)S(1)}) fusion(f32[2,128,1]{2,0,1:T(2,128)S(1)} %copy.2709, f32[2,128,128]{2,0,1:T(2,128)S(1)} %get-tuple-element.47, f32[2,128,1]{2,0,1:T(2,128)S(1)} %copy.2710, f32[2,128,128]{2,0,1:T(2,128)S(1)} %get-tuple-element.45, ...), kind=kLoop, calls=%fused_computation.75 | loop fusion | flops 1254912 | bytes 795648 | tf_op jit(solution)/shard_map/sub | solution.py:54
  67.6 1.7 %fusion.25 = f32[2,128,129]{2,0,1:T(2,128)S(1)} fusion(f32[2,128,129]{2,0,1:T(2,128)S(1)} %get-tuple-element.38, f32[2,128,129]{2,0,1:T(2,128)S(1)} %get-tuple-element.39, f32[2,128,1]{2,0,1:T(2,128)S(1)} %copy.2709, f32[2,128,128]{2,0,1:T(2,128)S(1)} %get-tuple-element.47, f32[2,128,1]{2,0,1:T(2,128)S(1)} %copy.2710, ...), kind=kLoop, calls=%fused_computation.105 | loop fusion | flops 693504 | bytes 662528 | tf_op jit(solution)/shard_map/sub | solution.py:51
  69.2 2.1 %multiply_subtract_fusion.1 = f32[2,128,129]{2,0,1:T(2,128)S(1)} fusion(f32[2,128,129]{2,0,1:T(2,128)S(1)} %get-tuple-element.39, f32[2,128,129]{2,0,1:T(2,128)S(1)} %get-tuple-element.38, f32[2,128,1]{2,0,1:T(2,128)S(1)} %copy.2719, f32[2,128,128]{2,0,1:T(2,128)S(1)} %div.119, f32[2,128,1]{2,0,1:T(2,128)S(1)} %copy.2718, f32[2,128,1]{2,0,1:T(2,128)S(1)} %copy.2709, ...), kind=kLoop, calls=%fused_computation.102 | loop fusion | flops 957696 | bytes 795648 | tf_op jit(solution)/shard_map/sub | solution.py:57
  72.8 1.9 %fusion.197 = (f32[2,128,128]{2,0,1:T(2,128)S(1)}, f32[2,128,128]{2,0,1:T(2,128)S(1)}, f32[2,128,128]{2,0,1:T(2,128)S(1)}, f32[2,128,128]{2,0,1:T(2,128)S(1)}) fusion(f32[2,128,128]{2,0,1:T(2,128)S(1)} %copy.2689, f32[2,128,128]{2,0,1:T(2,128)S(1)} %get-tuple-element.47, f32[2,129,128]{2,0,1:T(2,128)S(1)} %get-tuple-element.60, ...), kind=kLoop, calls=%fused_computation.485 | loop fusion | flops 1605632 | bytes 3149824 | tf_op jit(solution)/shard_map/div | solution.py:138
  76.4 1.3 %collective-permute-start.7 = (f32[3,2,128]{2,1,0:T(2,128)S(1)}, f32[3,2,128]{2,1,0:T(2,128)S(1)}, u32[]{:S(2)}, u32[]{:S(2)}) collective-permute-start(f32[3,2,128]{2,1,0:T(2,128)S(1)} %bitcast.389), channel_id=1, source_target_pairs={{4,0},{8,4},{12,8},{5,1},{9,5},{13,9},{6,2},{10,6},{14,10},{7,3},{... | collective-permute-start | bytes 9224 | tf_op jit(solution)/shard_map/ppermute | solution.py:23
  77.8 4.8 %collective-permute-start.6 = (f32[3,2,128]{2,1,0:T(2,128)S(1)}, f32[3,2,128]{2,1,0:T(2,128)S(1)}, u32[]{:S(2)}, u32[]{:S(2)}) collective-permute-start(f32[3,2,128]{2,1,0:T(2,128)S(1)} %bitcast.387), channel_id=1, source_target_pairs={{0,4},{4,8},{8,12},{1,5},{5,9},{9,13},{2,6},{6,10},{10,14},{3,7},{... | collective-permute-start | bytes 9224 | tf_op jit(solution)/shard_map/ppermute | solution.py:23
  83.9 5.5 %all_gather.15 = f32[4,3,8,128]{3,0,1,2:T(4,128)S(1)} all-gather(f32[4,3,2,128]{3,0,1,2:T(4,128)S(1)} %copy.2724), channel_id=1, replica_groups=mesh['region'=2,'tile'=4,'sub'=2,'lane'=2] {'sub','lane'}, dimensions={2}, use_global_device_ids=true | all-gather | bytes 61440 | tf_op jit(solution)/shard_map/all_gather | solution.py:162
  91.4 2.3 %fusion.19 = (f32[2,128,129]{2,0,1:T(2,128)S(1)}, f32[2,128,129]{2,0,1:T(2,128)S(1)}, f32[2,128,129]{2,0,1:T(2,128)S(1)}) fusion(f32[2,128,1]{2,0,1:T(2,128)S(1)} %copy.2733, f32[2,128,128]{2,0,1:T(2,128)S(1)} %get-tuple-element.35, f32[2,128,1]{2,0,1:T(2,128)S(1)} %copy.2734, f32[2,128,128]{2,0,1:T(2,128)S(1)} %get-tuple-element.33, ...), kind=kLoop, calls=%fused_computation.80 | loop fusion | flops 1254912 | bytes 795648 | tf_op jit(solution)/shard_map/sub | solution.py:54
  93.8 1.7 %fusion.23 = f32[2,128,129]{2,0,1:T(2,128)S(1)} fusion(f32[2,128,129]{2,0,1:T(2,128)S(1)} %get-tuple-element.26, f32[2,128,129]{2,0,1:T(2,128)S(1)} %get-tuple-element.27, f32[2,128,1]{2,0,1:T(2,128)S(1)} %copy.2733, f32[2,128,128]{2,0,1:T(2,128)S(1)} %get-tuple-element.35, f32[2,128,1]{2,0,1:T(2,128)S(1)} %copy.2734, ...), kind=kLoop, calls=%fused_computation.98 | loop fusion | flops 693504 | bytes 662528 | tf_op jit(solution)/shard_map/sub | solution.py:51
  95.4 2.1 %multiply_subtract_fusion = f32[2,128,129]{2,0,1:T(2,128)S(1)} fusion(f32[2,128,129]{2,0,1:T(2,128)S(1)} %get-tuple-element.27, f32[2,128,129]{2,0,1:T(2,128)S(1)} %get-tuple-element.26, f32[2,128,1]{2,0,1:T(2,128)S(1)} %copy.2743, f32[2,128,128]{2,0,1:T(2,128)S(1)} %div.131, f32[2,128,1]{2,0,1:T(2,128)S(1)} %copy.2742, f32[2,128,1]{2,0,1:T(2,128)S(1)} %copy.2733, ...), kind=kLoop, calls=%fused_computation.95 | loop fusion | flops 957696 | bytes 795648 | tf_op jit(solution)/shard_map/sub | solution.py:57
  99.0 1.9 %fusion.194 = (f32[2,128,128]{2,0,1:T(2,128)S(1)}, f32[2,128,128]{2,0,1:T(2,128)S(1)}, f32[2,128,128]{2,0,1:T(2,128)S(1)}, f32[2,128,128]{2,0,1:T(2,128)S(1)}) fusion(f32[2,128,128]{2,0,1:T(2,128)S(1)} %copy.2689, f32[2,128,128]{2,0,1:T(2,128)S(1)} %get-tuple-element.35, f32[2,129,128]{2,0,1:T(2,128)S(1)} %get-tuple-element.58, ...), kind=kLoop, calls=%fused_computation.484 | loop fusion | flops 1605632 | bytes 3149824 | tf_op jit(solution)/shard_map/div | solution.py:138
  (163 shorter events, 27.4 us)
Async XLA Ops:
  0.0 7.7 %copy-start = (bf16[2,4,128,128]{3,2,1,0:T(8,128)(2,1)S(1)}, bf16[2,4,128,128]{3,2,1,0:T(8,128)(2,1)}, u32[]{:S(2)}) copy-start(bf16[2,4,128,128]{3,2,1,0:T(8,128)(2,1)} %param.21) | copy-start | bytes 786436
  0.8 15.4 %collective-permute-start.1 = (f32[3,2,128]{2,1,0:T(2,128)S(1)}, f32[3,2,128]{2,1,0:T(2,128)S(1)}, u32[]{:S(2)}, u32[]{:S(2)}) collective-permute-start(f32[3,2,128]{2,1,0:T(2,128)S(1)} %bitcast.397), channel_id=1, source_target_pairs={{4,0},{8,4},{12,8},{5,1},{9,5},{13,9},{6,2},{10,6},{14,10},{7,3},{... | collective-permute-start | bytes 9224 | tf_op jit(solution)/shard_map/ppermute | solution.py:23
  2.1 5.6 %copy-start.6 = (s32[4]{0:T(128)S(1)}, s32[4]{0:T(128)}, u32[]{:S(2)}) copy-start(s32[4]{0:T(128)} %param.25) | copy-start | bytes 52
  2.1 14.1 %collective-permute-start = (f32[3,2,128]{2,1,0:T(2,128)S(1)}, f32[3,2,128]{2,1,0:T(2,128)S(1)}, u32[]{:S(2)}, u32[]{:S(2)}) collective-permute-start(f32[3,2,128]{2,1,0:T(2,128)S(1)} %bitcast.396), channel_id=1, source_target_pairs={{0,4},{4,8},{8,12},{1,5},{5,9},{9,13},{2,6},{6,10},{10,14},{3,7},{... | collective-permute-start | bytes 9224 | tf_op jit(solution)/shard_map/ppermute | solution.py:23
  8.7 4.4 %copy-start.5 = (s32[2,2,4]{2,1,0:T(2,128)S(1)}, s32[2,2,4]{2,1,0:T(2,128)}, u32[]{:S(2)}) copy-start(s32[2,2,4]{2,1,0:T(2,128)} %param.23) | copy-start | bytes 196
  8.7 4.7 %copy-start.1 = (f32[3,2,128,128]{3,2,1,0:T(8,128)S(1)}, f32[3,2,128,128]{3,2,1,0:T(8,128)}, u32[]{:S(2)}) copy-start(f32[3,2,128,128]{3,2,1,0:T(8,128)} %param.19) | copy-start | bytes 1179652
  8.7 13.3 %all-to-all-start = ((bf16[2,4,128,128]{3,2,0,1:T(8,128)(2,1)}), bf16[2,4,128,128]{3,2,0,1:T(8,128)(2,1)S(1)}, u32[]{:S(2)}, u32[]{:S(2)}) async-start(bf16[2,4,128,128]{3,2,0,1:T(8,128)(2,1)} %copy.2654), calls=%async_computation | async-start | bytes 524288 | tf_op jit(solution)/shard_map/all_to_all | solution.py:181
  13.9 0.7 copy-start.7
  15.0 0.9 copy-start.2
  23.1 6.8 %collective-permute-start.3 = (f32[1,2,128]{2,1,0:T(2,128)S(1)}, f32[1,2,128]{2,1,0:T(2,128)S(1)}, u32[]{:S(2)}, u32[]{:S(2)}) collective-permute-start(f32[1,2,128]{2,1,0:T(2,128)S(1)} %bitcast.399), channel_id=1, source_target_pairs={{4,0},{8,4},{12,8},{5,1},{9,5},{13,9},{6,2},{10,6},{14,10},{7,3},{... | collective-permute-start | bytes 3080 | tf_op jit(solution)/shard_map/ppermute | solution.py:23
  24.4 5.8 %collective-permute-start.2 = (f32[1,2,128]{2,1,0:T(2,128)S(1)}, f32[1,2,128]{2,1,0:T(2,128)S(1)}, u32[]{:S(2)}, u32[]{:S(2)}) collective-permute-start(f32[1,2,128]{2,1,0:T(2,128)S(1)} %bitcast.398), channel_id=1, source_target_pairs={{0,4},{4,8},{8,12},{1,5},{5,9},{9,13},{2,6},{6,10},{10,14},{3,7},{... | collective-permute-start | bytes 3080 | tf_op jit(solution)/shard_map/ppermute | solution.py:23
  36.1 0.7 copy-start.4
  36.8 0.7 copy-start.3
  50.3 7.1 %collective-permute-start.5 = (f32[3,2,128]{2,1,0:T(2,128)S(1)}, f32[3,2,128]{2,1,0:T(2,128)S(1)}, u32[]{:S(2)}, u32[]{:S(2)}) collective-permute-start(f32[3,2,128]{2,1,0:T(2,128)S(1)} %bitcast.388), channel_id=1, source_target_pairs={{4,0},{8,4},{12,8},{5,1},{9,5},{13,9},{6,2},{10,6},{14,10},{7,3},{... | collective-permute-start | bytes 9224 | tf_op jit(solution)/shard_map/ppermute | solution.py:23
  51.6 6.1 %collective-permute-start.4 = (f32[3,2,128]{2,1,0:T(2,128)S(1)}, f32[3,2,128]{2,1,0:T(2,128)S(1)}, u32[]{:S(2)}, u32[]{:S(2)}) collective-permute-start(f32[3,2,128]{2,1,0:T(2,128)S(1)} %bitcast.386), channel_id=1, source_target_pairs={{0,4},{4,8},{8,12},{1,5},{5,9},{9,13},{2,6},{6,10},{10,14},{3,7},{... | collective-permute-start | bytes 9224 | tf_op jit(solution)/shard_map/ppermute | solution.py:23
  76.4 7.1 %collective-permute-start.7 = (f32[3,2,128]{2,1,0:T(2,128)S(1)}, f32[3,2,128]{2,1,0:T(2,128)S(1)}, u32[]{:S(2)}, u32[]{:S(2)}) collective-permute-start(f32[3,2,128]{2,1,0:T(2,128)S(1)} %bitcast.389), channel_id=1, source_target_pairs={{4,0},{8,4},{12,8},{5,1},{9,5},{13,9},{6,2},{10,6},{14,10},{7,3},{... | collective-permute-start | bytes 9224 | tf_op jit(solution)/shard_map/ppermute | solution.py:23
  77.8 6.1 %collective-permute-start.6 = (f32[3,2,128]{2,1,0:T(2,128)S(1)}, f32[3,2,128]{2,1,0:T(2,128)S(1)}, u32[]{:S(2)}, u32[]{:S(2)}) collective-permute-start(f32[3,2,128]{2,1,0:T(2,128)S(1)} %bitcast.387), channel_id=1, source_target_pairs={{0,4},{4,8},{8,12},{1,5},{5,9},{9,13},{2,6},{6,10},{10,14},{3,7},{... | collective-permute-start | bytes 9224 | tf_op jit(solution)/shard_map/ppermute | solution.py:23
where the time goes:
time: 104 us; the launch traced here: 103 us
  other arithmetic  31.7 us (30%)
  starting transfers between devices  29.4 us (28%)
  blocking collectives  21.5 us (21%)
  local copies, waits for them, and re-layouts  15 us (14%)
  matrix products  2.67 us (3%)
  between operations  1.44 us (1%)
    ppermute x8, starting transfers between devices, from_behind(): return lax.ppermute(array, axis, pairs)  24.9 us
    all_gather x4, blocking collectives, route_faces(): arrived = lax.all_gather(pooled, ('sub', 'lane'), axis=2, tiled=True)  21.5 us
    sub x6, other arithmetic, face_flux(): 0.5 * (push_left + push_right)  9.15 us
    sub x6, other arithmetic, face_flux(): 0.5 * (held_left * speed_left * drift_left + held_right * speed_right * d...  8.54 us
    div x6, other arithmetic, advance(): return (depth_new, along_new / damping, cross_new / damping)  6.24 us
    sub x3, other arithmetic, face_flux(): 0.5 * (held_left * speed_left + held_right * speed_right)  4.98 us
    all_to_all x1, starting transfers between devices, local(): lax.all_to_all(outbound, 'tile', split_axis=1, concat_axis=1, tiled=True)  4.43 us
    slice x9, local copies, waits for them, and re-layouts, face_strips(): fields[:, :, -1, :]  2.7 us
  transfers between devices with their start and end apart: 9, of which 3 were waited for; matrix products, arithmetic and copies ran while one was open for 6% of the time, Pallas kernels for 0%

commit v1 on v0

v1 whole, which is shorter than its diff:
```python
import functools

import jax
import jax.numpy as jnp
from jax import lax
from jax.experimental import pallas as pl
from jax.experimental.pallas import tpu as pltpu
from jax.sharding import PartitionSpec as P

STEPS = 3
GRAVITY = 9.81
CELL = 30.0
DT = 1.0
ROWS = 32
AXES = ("region", "tile", "sub", "lane")
MESH = pl.DeviceIdType.MESH


def root(x):
    return x * lax.rsqrt(jnp.maximum(x, 1.2e-38))


def face_flux(eta_l, z_l, n_l, t_l, eta_r, z_r, n_r, t_r):
    z_face = jnp.maximum(z_l, z_r)
    h_l = jnp.maximum(eta_l - z_face, 0.0)
    h_r = jnp.maximum(eta_r - z_face, 0.0)
    wave = jnp.maximum(
        jnp.abs(n_l) + root(GRAVITY * h_l), jnp.abs(n_r) + root(GRAVITY * h_r)
    )
    m_l = h_l * n_l
    m_r = h_r * n_r
    d = h_r - h_l
    mass = (m_l + m_r) - wave * d
    base = (m_l * n_l + m_r * n_r) - wave * (m_r - m_l)
    press = (0.5 * GRAVITY) * d * (h_r + h_l)
    tang = (m_l * t_l + m_r * t_r) - wave * (h_r * t_r - h_l * t_l)
    return mass, base, press, tang


def kernel(
    sizes,
    wet_ref,
    links_ref,
    source_ref,
    target_ref,
    state_ref,
    local_ref,
    store_ref,
    out_ref,
    out_bed,
    out_rough,
    in_bed,
    in_rough,
    bed,
    drag,
    fields,
    prim,
    faces,
    tend,
    columns,
    rim,
    rim_t,
    own,
    ghost,
    msgs,
    strips_x,
    strips_n,
    strips_s,
    terrain_send,
    terrain_recv,
    strip_send,
    strip_recv,
):
    bands, subs, lanes, slots, size = sizes
    peers = subs * lanes
    band = lax.axis_index("tile")
    peer = lax.axis_index("sub") * lanes + lax.axis_index("lane")
    has_north = band > 0
    has_south = band < bands - 1

    def place(to_band, to_peer):
        return {"tile": to_band, "sub": to_peer // lanes, "lane": to_peer % lanes}

    barrier = pltpu.get_barrier_semaphore()

    def greet(to_band, to_peer):
        pl.semaphore_signal(
            barrier, inc=1, device_id=place(to_band, to_peer), device_id_type=MESH
        )

    for offset in range(1, peers):
        greet(band, lax.rem(peer + offset, peers))
    for offset in range(1, bands):
        greet(lax.rem(band + offset, bands), peer)

    @pl.when(has_north)
    def _():
        for offset in range(1, peers):
            greet(band - 1, lax.rem(peer + offset, peers))

    @pl.when(has_south)
    def _():
        for offset in range(1, peers):
            greet(band + 1, lax.rem(peer + offset, peers))

    for r in range(bands):
        block = jnp.int32(0)
        for j in range(bands):
            block = jnp.where(target_ref[j] == r, j, block)
        out_bed[r] = store_ref[0, block]
        out_rough[r] = store_ref[1, block]
    in_bed[band] = out_bed[band]
    in_rough[band] = out_rough[band]

    count = (peers - 1) + (bands - 1)
    count = count + jnp.where(has_north, peers - 1, 0) + jnp.where(has_south, peers - 1, 0)
    pl.semaphore_wait(barrier, count)

    for part, (source, target) in enumerate(((out_bed, in_bed), (out_rough, in_rough))):
        for offset in range(1, bands):
            to_band = lax.rem(band + offset, bands)
            pltpu.make_async_remote_copy(
                src_ref=source.at[to_band],
                dst_ref=target.at[band],
                send_sem=terrain_send.at[part],
                recv_sem=terrain_recv.at[part],
                device_id=place(to_band, peer),
                device_id_type=MESH,
            ).start()

    def wait_for(ref, length, sem):
        view = ref.at[pl.ds(0, length)]
        pltpu.make_async_copy(view, view, sem).wait()

    chunks = size // ROWS
    lane_id = lax.broadcasted_iota(jnp.int32, (ROWS, size), 1)

    def edge_columns(t, rows, q, value, before):
        rolled = pltpu.roll(value, 1 + 2 * q, axis=1)
        return jnp.where(lane_id // 2 == q, rolled, before)

    for q in range(3):
        for t in range(slots):
            prim[q, t, pl.ds(size, 8)] = jnp.zeros((8, size), jnp.float32)
    for t in range(slots):
        bed[t, pl.ds(size, 8)] = jnp.zeros((8, size), jnp.float32)
        rim[t] = jnp.zeros((size, size), jnp.float32)

    wait_for(in_bed, bands - 1, terrain_recv.at[0])

    for t in range(slots):
        fetched = in_bed[jnp.maximum(source_ref[t], 0)].astype(jnp.float32)
        bed[t, pl.ds(0, size)] = jnp.where(
            source_ref[t] >= 0, fetched, local_ref[0, t].astype(jnp.float32)
        )

    def first(i, carry):
        t = i // chunks
        rows = pl.ds(pl.multiple_of((i % chunks) * ROWS, ROWS), ROWS)
        h = state_ref[0, t, rows]
        z = bed[t, rows]
        inv = 1.0 / h
        u = state_ref[1, t, rows] * inv
        v = state_ref[2, t, rows] * inv
        prim[0, t, rows] = h + z
        prim[1, t, rows] = u
        prim[2, t, rows] = v
        value = edge_columns(t, rows, 0, h, jnp.zeros_like(h))
        value = edge_columns(t, rows, 1, u, value)
        value = edge_columns(t, rows, 2, v, value)
        columns[t, rows] = edge_columns(t, rows, 3, z, value)
        return carry

    lax.fori_loop(0, slots * chunks, first, 0)

    def send_strips(step):
        current = state_ref if step == 0 else fields
        for t in range(slots):
            turned = jnp.transpose(columns[t])
            for q in range(4):
                if q == 3 and step > 0:
                    for f in range(4):
                        msgs[step, f, pl.ds(4 * t + 3, 1)] = own[3, pl.ds(f * slots + t, 1)]
                    continue
                if q == 0:
                    top, low = current[0, t, pl.ds(0, 1)], current[0, t, pl.ds(size - 1, 1)]
                elif q == 3:
                    top, low = bed[t, pl.ds(0, 1)], bed[t, pl.ds(size - 1, 1)]
                else:
                    top, low = prim[q, t, pl.ds(0, 1)], prim[q, t, pl.ds(size - 1, 1)]
                strip = (turned[2 * q + 1 : 2 * q + 2], turned[2 * q : 2 * q + 1], top, low)
                for f in range(4):
                    msgs[step, f, pl.ds(4 * t + q, 1)] = strip[f]
                    own[q, pl.ds(f * slots + t, 1)] = strip[f]
        strips_x[step][peer] = msgs[step, pl.ds(0, 2)]

        def send(kind, source, target, to_band, to_peer):
            pltpu.make_async_remote_copy(
                src_ref=source,
                dst_ref=target.at[peer],
                send_sem=strip_send.at[step, kind],
                recv_sem=strip_recv.at[step, kind],
                device_id=place(to_band, to_peer),
                device_id_type=MESH,
            ).start()

        @pl.when(has_south)
        def _():
            for offset in range(peers):
                to_peer = lax.rem(peer + offset, peers)
                send(1, msgs.at[step, 3], strips_n[step], band + 1, to_peer)

        @pl.when(has_north)
        def _():
            for offset in range(peers):
                to_peer = lax.rem(peer + offset, peers)
                send(2, msgs.at[step, 2], strips_s[step], band - 1, to_peer)

        for offset in range(1, peers):
            to_peer = lax.rem(peer + offset, peers)
            send(0, msgs.at[step, pl.ds(0, 2)], strips_x[step], band, to_peer)

    def inner(i, carry):
        t = i // chunks
        start = pl.multiple_of((i % chunks) * ROWS, ROWS)
        rows = pl.ds(start, ROWS)
        below = pl.ds(start + 1, ROWS)
        eta, u, v, z = prim[0, t, rows], prim[1, t, rows], prim[2, t, rows], bed[t, rows]
        east = [pltpu.roll(x, size - 1, axis=1) for x in (eta, z, u, v)]
        mass, base, press, tang = face_flux(eta, z, u, v, *east)
        inside = lane_id < size - 1
        mass = jnp.where(inside, mass, 0.0)
        far = jnp.where(inside, base + press, 0.0)
        near = jnp.where(inside, base - press, 0.0)
        tang = jnp.where(inside, tang, 0.0)
        tend[0, t, rows] = mass - pltpu.roll(mass, 1, axis=1)
        tend[1, t, rows] = far - pltpu.roll(near, 1, axis=1)
        tend[2, t, rows] = tang - pltpu.roll(tang, 1, axis=1)
        mass, base, press, tang = face_flux(
            eta, z, v, u, prim[0, t, below], bed[t, below], prim[2, t, below], prim[1, t, below]
        )
        into = pl.ds(pl.multiple_of(start + 8, 8), ROWS)
        faces[0, t, into] = mass
        faces[1, t, into] = base + press
        faces[2, t, into] = base - press
        faces[3, t, into] = tang
        return carry

    def wait_strips(step):
        if peers > 1:
            wait_for(strips_x[step], peers - 1, strip_recv.at[step, 0])

        @pl.when(has_north)
        def _():
            wait_for(strips_n[step], peers, strip_recv.at[step, 1])

        @pl.when(has_south)
        def _():
            wait_for(strips_s[step], peers, strip_recv.at[step, 2])

    def rims(step):
        for t in range(slots):
            for f in range(4):
                device = links_ref[t, 0, f]
                linked = device >= 0
                who = lax.rem(jnp.maximum(device, 0), peers)
                rows = pl.ds(4 * jnp.maximum(links_ref[t, 1, f], 0), 4)
                if f < 2:
                    remote = strips_x[step][who, 1 - f, rows]
                else:
                    remote = (strips_n if f == 2 else strips_s)[step][who, rows]
                row = pl.ds(f * slots + t, 1)
                for q in range(4):
                    mine = own[q, row]
                    if q == (1 if f < 2 else 2):
                        mine = -mine
                    ghost[q, row] = jnp.where(linked, remote[q : q + 1], mine)
        row_id = lax.broadcasted_iota(jnp.int32, (4 * slots, size), 0) // slots
        near_side = row_id % 2 == 0
        across = row_id < 2
        g = [ghost[q] for q in range(4)]
        o = [own[q] for q in range(4)]

        def ordered(x):
            h, u, v, z = x
            return h + z, z, jnp.where(across, u, v), jnp.where(across, v, u)

        go, oo = ordered(g), ordered(o)
        left = [jnp.where(near_side, a, b) for a, b in zip(go, oo)]
        right = [jnp.where(near_side, b, a) for a, b in zip(go, oo)]
        mass, base, press, tang = face_flux(*left, *right)
        normal = jnp.where(near_side, base - press, base + press)

        def pick(value, f, t):
            return value[f * slots + t : f * slots + t + 1]

        for t in range(slots):
            for q, value in enumerate((mass, normal, tang)):
                rim[t, pl.ds(2 * q, 1)] = pick(value, 1, t)
                rim[t, pl.ds(2 * q + 1, 1)] = -pick(value, 0, t)
            top, low = pl.ds(7, 1), pl.ds(7 + size, 1)
            faces[0, t, top] = pick(mass, 2, t)
            faces[2, t, top] = pick(normal, 2, t)
            faces[3, t, top] = pick(tang, 2, t)
            faces[0, t, low] = pick(mass, 3, t)
            faces[1, t, low] = pick(normal, 3, t)
            faces[3, t, low] = pick(tang, 3, t)
            rim_t[t] = jnp.transpose(rim[t])

    def update(step, i, carry):
        last = step == STEPS - 1
        current = state_ref if step == 0 else fields
        t = i // chunks
        start = pl.multiple_of((i % chunks) * ROWS, ROWS)
        rows = pl.ds(start, ROWS)
        here = pl.ds(pl.multiple_of(start + 8, 8), ROWS)
        above = pl.ds(start + 7, ROWS)
        turned = rim_t[t, rows]
        border = (lane_id == 0) | (lane_id == size - 1)

        def sides(q):
            return jnp.where(border, pltpu.roll(turned, size - 1 - 2 * q, axis=1), 0.0)

        ratio = 0.5 * DT / CELL
        h = current[0, t, rows] - ratio * (
            tend[0, t, rows] + sides(0) + (faces[0, t, here] - faces[0, t, above])
        )
        qx = current[1, t, rows] - ratio * (
            tend[1, t, rows] + sides(1) + (faces[3, t, here] - faces[3, t, above])
        )
        qy = current[2, t, rows] - ratio * (
            tend[2, t, rows] + sides(2) + (faces[1, t, here] - faces[2, t, above])
        )
        power = jnp.exp((-7.0 / 3.0) * jnp.log(h))
        damp = 1.0 / (1.0 + drag[t, rows] * root(qx * qx + qy * qy) * power)
        qx = qx * damp
        qy = qy * damp
        if last:
            live = t < wet_ref[0]
            out_ref[0, t, rows] = jnp.where(live, h, 0.0)
            out_ref[1, t, rows] = jnp.where(live, qx, 0.0)
            out_ref[2, t, rows] = jnp.where(live, qy, 0.0)
        else:
            fields[0, t, rows] = h
            fields[1, t, rows] = qx
            fields[2, t, rows] = qy
            inv = 1.0 / h
            u = qx * inv
            v = qy * inv
            prim[0, t, rows] = h + bed[t, rows]
            prim[1, t, rows] = u
            prim[2, t, rows] = v
            value = edge_columns(t, rows, 0, h, jnp.zeros_like(h))
            value = edge_columns(t, rows, 1, u, value)
            columns[t, rows] = edge_columns(t, rows, 2, v, value)
        return carry

    for step in range(STEPS):
        send_strips(step)
        lax.fori_loop(0, slots * chunks, inner, 0)
        if step == 0:
            wait_for(in_rough, bands - 1, terrain_recv.at[1])
            for t in range(slots):
                fetched = in_rough[jnp.maximum(source_ref[t], 0)].astype(jnp.float32)
                rough = jnp.where(
                    source_ref[t] >= 0, fetched, local_ref[1, t].astype(jnp.float32)
                )
                drag[t] = (DT * GRAVITY) * rough * rough
        wait_strips(step)
        rims(step)
        lax.fori_loop(0, slots * chunks, functools.partial(update, step), 0)

    for part, source in enumerate((out_bed, out_rough)):
        wait_for(source, bands - 1, terrain_send.at[part])
    for step in range(STEPS):
        wait_for(strips_x[step], peers - 1, strip_send.at[step, 0])

        @pl.when(has_south)
        def _():
            wait_for(strips_n[step], peers, strip_send.at[step, 1])

        @pl.when(has_north)
        def _():
            wait_for(strips_s[step], peers, strip_send.at[step, 2])


def local(sizes, state, terrain_local, terrain_store, wet_count, face_links, new_source, store_target):
    bands, subs, lanes, slots, size = sizes
    peers = subs * lanes
    f32, bf16 = jnp.float32, jnp.bfloat16
    block = (bands, size, size)
    smem = pl.BlockSpec(memory_space=pltpu.SMEM)
    vmem = pl.BlockSpec(memory_space=pltpu.VMEM)
    msg = (4 * slots, size)
    return pl.pallas_call(
        functools.partial(kernel, sizes),
        out_shape=jax.ShapeDtypeStruct(state.shape, f32),
        in_specs=[smem] * 4 + [vmem] * 3,
        out_specs=vmem,
        scratch_shapes=[
            pltpu.VMEM(block, bf16),
            pltpu.VMEM(block, bf16),
            pltpu.VMEM(block, bf16),
            pltpu.VMEM(block, bf16),
            pltpu.VMEM((slots, size + 8, size), f32),
            pltpu.VMEM((slots, size, size), f32),
            pltpu.VMEM((3, slots, size, size), f32),
            pltpu.VMEM((3, slots, size + 8, size), f32),
            pltpu.VMEM((4, slots, size + 16, size), f32),
            pltpu.VMEM((3, slots, size, size), f32),
            pltpu.VMEM((slots, size, size), f32),
            pltpu.VMEM((slots, size, size), f32),
            pltpu.VMEM((slots, size, size), f32),
            pltpu.VMEM((4,) + msg, f32),
            pltpu.VMEM((4,) + msg, f32),
            pltpu.VMEM((STEPS, 4) + msg, f32),
            [pltpu.VMEM((peers, 2) + msg, f32) for _ in range(STEPS)],
            [pltpu.VMEM((peers,) + msg, f32) for _ in range(STEPS)],
            [pltpu.VMEM((peers,) + msg, f32) for _ in range(STEPS)],
            pltpu.SemaphoreType.DMA((2,)),
            pltpu.SemaphoreType.DMA((2,)),
            pltpu.SemaphoreType.DMA((STEPS, 3)),
            pltpu.SemaphoreType.DMA((STEPS, 3)),
        ],
        compiler_params=pltpu.CompilerParams(
            collective_id=0, has_side_effects=True, vmem_limit_bytes=32 * 1024 * 1024
        ),
    )(wet_count, face_links, new_source, store_target, state, terrain_local, terrain_store)


def solution(mesh):
    shape = mesh.shape
    devices = P(None, AXES, None, None)
    flat = P(AXES)

    def whole(state, *rest):
        def part(block, *others):
            sizes = (shape["tile"], shape["sub"], shape["lane"], block.shape[1], block.shape[2])
            return local(sizes, block, *others)

        return jax.shard_map(
            part,
            mesh=mesh,
            in_specs=(devices, devices, devices, flat, P(AXES, None, None), flat, flat),
            out_specs=devices,
            check_vma=False,
        )(state, *rest)

    return whole
```

time: 104 us -> 32 us (0.31); the launches traced: 103 us -> 31.8 us
  other arithmetic: 31.7 us -> 0 us
  starting transfers between devices: 29.4 us -> 0 us
  Pallas kernels: 0 us -> 26.8 us
  blocking collectives: 21.5 us -> 0 us
  local copies, waits for them, and re-layouts: 15 us -> 4.28 us
  matrix products: 2.67 us -> 0 us
    pallas_call x0 -> x1, Pallas kernels: none -> 26.8 us  [local(): pl.pallas_call(functools.partial(kernel, sizes), out_shape=jax.ShapeDtype...]
    ppermute x8 -> x0, starting transfers between devices: 24.9 us -> none  [from_behind(): return lax.ppermute(array, axis, pairs)]
    sub x15 -> x0, other arithmetic: 22.7 us -> none  [the longest x6 9.15 us: face_flux(): 0.5 * (push_left + push_right)]
    all_gather x4 -> x0, blocking collectives: 21.5 us -> none  [route_faces(): arrived = lax.all_gather(pooled, ('sub', 'lane'), axis=2, tiled=True)]
    div x6 -> x0, other arithmetic: 6.24 us -> none  [advance(): return (depth_new, along_new / damping, cross_new / damping)]
    slice x25 -> x0, local copies, waits for them, and re-layouts: 5.57 us -> none  [the longest x9 2.7 us: face_strips(): fields[:, :, -1, :]]
    all_to_all x1 -> x0, starting transfers between devices: 4.43 us -> none  [local(): lax.all_to_all(outbound, 'tile', split_axis=1, concat_axis=1, tiled=True)]
    another operation x44 -> x0, local copies, waits for them, and re-layouts: 4.26 us -> none  [the longest x15 1.9 us: across(): west_side[field_index][:, :, None]]
  transfers between devices with their start and end apart: 9 -> 0, of which waited for: 3 -> 0; matrix products, arithmetic and copies ran while one was open for 6% -> 0% of each run, Pallas kernels for 0% -> 0%
where the time goes in v1:
time: 32 us; the launch traced here: 31.8 us
  Pallas kernels  26.8 us (84%)
  local copies, waits for them, and re-layouts  4.28 us (13%)
  between operations  0.72 us (2%)
    pallas_call x1, Pallas kernels, local(): pl.pallas_call(functools.partial(kernel, sizes), out_shape=jax.ShapeDtype...  26.8 us
    unnamed x13, local copies, waits for them, and re-layouts  4.28 us

profile of v1, /device:TPU:0, one launch (start us, length us, event | category | flops | bytes accessed | tf_op | source)
XLA Modules:
  0.0 31.8 jit_solution(1792396303154778742)
XLA Ops:
  0.0 0.0 copy-start.5
  0.0 0.0 copy-start.4
  0.7 0.0 copy-done.5
  0.7 0.0 copy-done.4
  0.7 0.0 copy-start
  0.7 1.0 %copy-done = f32[3,2,128,128]{3,2,1,0:T(8,128)S(1)} copy-done((f32[3,2,128,128]{3,2,1,0:T(8,128)S(1)}, f32[3,2,128,128]{3,2,1,0:T(8,128)}, u32[]{:S(2)}) %copy-start) | copy-done | bytes 393240
  1.7 0.0 copy-start.1
  1.7 0.9 %copy-done.1 = bf16[2,4,128,128]{3,2,1,0:T(8,128)(2,1)S(1)} copy-done((bf16[2,4,128,128]{3,2,1,0:T(8,128)(2,1)S(1)}, bf16[2,4,128,128]{3,2,1,0:T(8,128)(2,1)}, u32[]{:S(2)}) %copy-start.1) | copy-done | bytes 262168
  2.7 0.0 copy-start.2
  2.7 0.9 %copy-done.2 = bf16[2,2,128,128]{3,2,1,0:T(8,128)(2,1)S(1)} copy-done((bf16[2,2,128,128]{3,2,1,0:T(8,128)(2,1)S(1)}, bf16[2,2,128,128]{3,2,1,0:T(8,128)(2,1)}, u32[]{:S(2)}) %copy-start.2) | copy-done | bytes 131096
  3.6 0.0 copy-start.3
  3.6 0.7 %copy-done.3 = s32[2,2,4]{2,1,0:T(2,128)S(1)} copy-done((s32[2,2,4]{2,1,0:T(2,128)S(1)}, s32[2,2,4]{2,1,0:T(2,128)}, u32[]{:S(2)}) %copy-start.3) | copy-done | bytes 88
  4.2 26.8 %shard_map.73 = f32[3,2,128,128]{3,2,1,0:T(8,128)S(1)} custom-call(s32[1]{0:T(128)S(6)} %copy.9.wet_ref, s32[2,2,4]{2,1,0:T(2,128)S(1)} %copy-done.3, s32[2]{0:T(128)S(1)} %copy-done.4, s32[4]{0:T(128)S(1)} %copy-done.5, f32[3,2,128,128]{3,2,1,0:T(8,128)S(1)} %copy-done, bf16[2,2,128,128]{3,2,1,0:T(8,128)(2,1)S(1)} %copy-done.2, ...), custom_call_target="tpu_custom_call" | custom-call | tf_op jit(solution)/shard_map/pallas_call | solution.py:395
  31.0 0.7 %copy.10 = f32[3,2,128,128]{3,2,1,0:T(8,128)} copy(f32[3,2,128,128]{3,2,1,0:T(8,128)S(1)} %shard_map.73) | data formatting | bytes 786432
Async XLA Ops:
  0.0 0.7 %copy-start.5 = (s32[4]{0:T(128)S(1)}, s32[4]{0:T(128)}, u32[]{:S(2)}) copy-start(s32[4]{0:T(128)} %target_ref.1) | copy-start | bytes 52
  0.0 0.7 %copy-start.4 = (s32[2]{0:T(128)S(1)}, s32[2]{0:T(128)}, u32[]{:S(2)}) copy-start(s32[2]{0:T(128)} %source_ref.1) | copy-start | bytes 28
  0.7 1.0 %copy-start = (f32[3,2,128,128]{3,2,1,0:T(8,128)S(1)}, f32[3,2,128,128]{3,2,1,0:T(8,128)}, u32[]{:S(2)}) copy-start(f32[3,2,128,128]{3,2,1,0:T(8,128)} %state_ref.1) | copy-start | bytes 1179652
  1.7 0.9 %copy-start.1 = (bf16[2,4,128,128]{3,2,1,0:T(8,128)(2,1)S(1)}, bf16[2,4,128,128]{3,2,1,0:T(8,128)(2,1)}, u32[]{:S(2)}) copy-start(bf16[2,4,128,128]{3,2,1,0:T(8,128)(2,1)} %store_ref.1) | copy-start | bytes 786436
  2.7 0.9 %copy-start.2 = (bf16[2,2,128,128]{3,2,1,0:T(8,128)(2,1)S(1)}, bf16[2,2,128,128]{3,2,1,0:T(8,128)(2,1)}, u32[]{:S(2)}) copy-start(bf16[2,2,128,128]{3,2,1,0:T(8,128)(2,1)} %local_ref.1) | copy-start | bytes 393220
  3.6 0.7 %copy-start.3 = (s32[2,2,4]{2,1,0:T(2,128)S(1)}, s32[2,2,4]{2,1,0:T(2,128)}, u32[]{:S(2)}) copy-start(s32[2,2,4]{2,1,0:T(2,128)} %links_ref.1) | copy-start | bytes 196

commit v2 on v1

--- a/solution.py
+++ b/solution.py
@@ -11,7 +11,7 @@
 GRAVITY = 9.81
 CELL = 30.0
 DT = 1.0
-ROWS = 32
+ROWS = 128
 AXES = ("region", "tile", "sub", "lane")
 MESH = pl.DeviceIdType.MESH
 
@@ -39,6 +39,14 @@
 
 def kernel(
     sizes,
+    wet_hbm,
+    links_hbm,
+    source_hbm,
+    target_hbm,
+    state_hbm,
+    local_hbm,
+    store_hbm,
+    out_ref,
     wet_ref,
     links_ref,
     source_ref,
@@ -46,7 +54,6 @@
     state_ref,
     local_ref,
     store_ref,
-    out_ref,
     out_bed,
     out_rough,
     in_bed,
@@ -66,6 +73,9 @@
     strips_x,
     strips_n,
     strips_s,
+    edge_msgs,
+    edge_in,
+    load_sem,
     terrain_send,
     terrain_recv,
     strip_send,
@@ -73,13 +83,40 @@
 ):
     bands, subs, lanes, slots, size = sizes
     peers = subs * lanes
+    total = bands * peers
     band = lax.axis_index("tile")
     peer = lax.axis_index("sub") * lanes + lax.axis_index("lane")
+    me = band * peers + peer
     has_north = band > 0
     has_south = band < bands - 1
 
+    loads = [
+        pltpu.make_async_copy(source, target, load_sem.at[i])
+        for i, (source, target) in enumerate(
+            (
+                (target_hbm, target_ref),
+                (store_hbm, store_ref),
+                (source_hbm, source_ref),
+                (state_hbm, state_ref),
+                (local_hbm, local_ref),
+                (links_hbm, links_ref),
+                (wet_hbm, wet_ref),
+            )
+        )
+    ]
+    for load in loads:
+        load.start()
+
     def place(to_band, to_peer):
         return {"tile": to_band, "sub": to_peer // lanes, "lane": to_peer % lanes}
+
+    def each_other(body):
+        def one(offset, carry):
+            other = lax.rem(me + offset, total)
+            body(other // peers, other % peers)
+            return carry
+
+        lax.fori_loop(1, total, one, 0, unroll=total <= 16)
 
     barrier = pltpu.get_barrier_semaphore()
 
@@ -88,49 +125,52 @@
             barrier, inc=1, device_id=place(to_band, to_peer), device_id_type=MESH
         )
 
-    for offset in range(1, peers):
-        greet(band, lax.rem(peer + offset, peers))
-    for offset in range(1, bands):
-        greet(lax.rem(band + offset, bands), peer)
-
-    @pl.when(has_north)
-    def _():
-        for offset in range(1, peers):
-            greet(band - 1, lax.rem(peer + offset, peers))
-
-    @pl.when(has_south)
-    def _():
-        for offset in range(1, peers):
-            greet(band + 1, lax.rem(peer + offset, peers))
-
+    each_other(greet)
+
+    def wait_for(ref, length, sem):
+        view = ref.at[pl.ds(0, length)]
+        pltpu.make_async_copy(view, view, sem).wait()
+
+    wide_id = lax.broadcasted_iota(jnp.int32, (size, size), 1)
+
+    for q in range(3):
+        for t in range(slots):
+            prim[q, t, pl.ds(size, 8)] = jnp.zeros((8, size), jnp.float32)
+    for t in range(slots):
+        bed[t, pl.ds(size, 8)] = jnp.zeros((8, size), jnp.float32)
+        rim[t] = jnp.zeros((size, size), jnp.float32)
+    msgs[...] = jnp.zeros_like(msgs)
+    edge_msgs[...] = jnp.zeros_like(edge_msgs)
+
+    loads[0].wait()
+    loads[1].wait()
+    sides = jnp.zeros((size, size), jnp.float32)
     for r in range(bands):
         block = jnp.int32(0)
         for j in range(bands):
             block = jnp.where(target_ref[j] == r, j, block)
-        out_bed[r] = store_ref[0, block]
+        level = store_ref[0, block]
+        out_bed[r] = level
         out_rough[r] = store_ref[1, block]
+        level = level.astype(jnp.float32)
+        sides = jnp.where(wide_id // 2 == r, pltpu.roll(level, 1 + 2 * r, axis=1), sides)
+        if r > 0:
+            edge_msgs[r - 1, pl.ds(2, 1)] = level[0:1]
+        if r < bands - 1:
+            edge_msgs[r + 1, pl.ds(3, 1)] = level[size - 1 : size]
+    sides = jnp.transpose(sides)
+    loads[2].wait()
+    for r in range(bands):
+        edge_msgs[r, pl.ds(0, 1)] = sides[2 * r + 1 : 2 * r + 2]
+        edge_msgs[r, pl.ds(1, 1)] = sides[2 * r : 2 * r + 1]
+        for t in range(slots):
+            row = jnp.full((1, size), source_ref[t].astype(jnp.float32))
+            edge_msgs[r, pl.ds(4 + t, 1)] = row
     in_bed[band] = out_bed[band]
     in_rough[band] = out_rough[band]
-
-    count = (peers - 1) + (bands - 1)
-    count = count + jnp.where(has_north, peers - 1, 0) + jnp.where(has_south, peers - 1, 0)
-    pl.semaphore_wait(barrier, count)
-
-    for part, (source, target) in enumerate(((out_bed, in_bed), (out_rough, in_rough))):
-        for offset in range(1, bands):
-            to_band = lax.rem(band + offset, bands)
-            pltpu.make_async_remote_copy(
-                src_ref=source.at[to_band],
-                dst_ref=target.at[band],
-                send_sem=terrain_send.at[part],
-                recv_sem=terrain_recv.at[part],
-                device_id=place(to_band, peer),
-                device_id_type=MESH,
-            ).start()
-
-    def wait_for(ref, length, sem):
-        view = ref.at[pl.ds(0, length)]
-        pltpu.make_async_copy(view, view, sem).wait()
+    edge_in[me] = edge_msgs[band]
+    for load in loads[3:]:
+        load.wait()
 
     chunks = size // ROWS
     lane_id = lax.broadcasted_iota(jnp.int32, (ROWS, size), 1)
@@ -138,36 +178,20 @@
     def edge_columns(t, rows, q, value, before):
         rolled = pltpu.roll(value, 1 + 2 * q, axis=1)
         return jnp.where(lane_id // 2 == q, rolled, before)
-
-    for q in range(3):
-        for t in range(slots):
-            prim[q, t, pl.ds(size, 8)] = jnp.zeros((8, size), jnp.float32)
-    for t in range(slots):
-        bed[t, pl.ds(size, 8)] = jnp.zeros((8, size), jnp.float32)
-        rim[t] = jnp.zeros((size, size), jnp.float32)
-
-    wait_for(in_bed, bands - 1, terrain_recv.at[0])
-
-    for t in range(slots):
-        fetched = in_bed[jnp.maximum(source_ref[t], 0)].astype(jnp.float32)
-        bed[t, pl.ds(0, size)] = jnp.where(
-            source_ref[t] >= 0, fetched, local_ref[0, t].astype(jnp.float32)
-        )
 
     def first(i, carry):
         t = i // chunks
         rows = pl.ds(pl.multiple_of((i % chunks) * ROWS, ROWS), ROWS)
         h = state_ref[0, t, rows]
-        z = bed[t, rows]
         inv = 1.0 / h
         u = state_ref[1, t, rows] * inv
         v = state_ref[2, t, rows] * inv
-        prim[0, t, rows] = h + z
         prim[1, t, rows] = u
         prim[2, t, rows] = v
         value = edge_columns(t, rows, 0, h, jnp.zeros_like(h))
         value = edge_columns(t, rows, 1, u, value)
         value = edge_columns(t, rows, 2, v, value)
+        z = local_ref[0, t, rows].astype(jnp.float32)
         columns[t, rows] = edge_columns(t, rows, 3, z, value)
         return carry
 
@@ -179,13 +203,12 @@
             turned = jnp.transpose(columns[t])
             for q in range(4):
                 if q == 3 and step > 0:
-                    for f in range(4):
-                        msgs[step, f, pl.ds(4 * t + 3, 1)] = own[3, pl.ds(f * slots + t, 1)]
                     continue
                 if q == 0:
                     top, low = current[0, t, pl.ds(0, 1)], current[0, t, pl.ds(size - 1, 1)]
                 elif q == 3:
-                    top, low = bed[t, pl.ds(0, 1)], bed[t, pl.ds(size - 1, 1)]
+                    level = local_ref[0, t].astype(jnp.float32)
+                    top, low = level[0:1], level[size - 1 : size]
                 else:
                     top, low = prim[q, t, pl.ds(0, 1)], prim[q, t, pl.ds(size - 1, 1)]
                 strip = (turned[2 * q + 1 : 2 * q + 2], turned[2 * q : 2 * q + 1], top, low)
@@ -193,6 +216,8 @@
                     msgs[step, f, pl.ds(4 * t + q, 1)] = strip[f]
                     own[q, pl.ds(f * slots + t, 1)] = strip[f]
         strips_x[step][peer] = msgs[step, pl.ds(0, 2)]
+        if step == 0:
+            pl.semaphore_wait(barrier, total - 1)
 
         def send(kind, source, target, to_band, to_peer):
             pltpu.make_async_remote_copy(
@@ -264,13 +289,22 @@
                 device = links_ref[t, 0, f]
                 linked = device >= 0
                 who = lax.rem(jnp.maximum(device, 0), peers)
-                rows = pl.ds(4 * jnp.maximum(links_ref[t, 1, f], 0), 4)
+                slot = jnp.maximum(links_ref[t, 1, f], 0)
+                rows = pl.ds(4 * slot, 4)
                 if f < 2:
                     remote = strips_x[step][who, 1 - f, rows]
                 else:
                     remote = (strips_n if f == 2 else strips_s)[step][who, rows]
                 row = pl.ds(f * slots + t, 1)
-                for q in range(4):
+                if step == 0:
+                    at = band + (0, 0, -1, 1)[f]
+                    holder = edge_in[jnp.clip(at, 0, bands - 1) * peers + who, pl.ds(4 + slot, 1)]
+                    level = remote[3:4]
+                    for r in range(bands):
+                        edge = edge_in[r * peers + who, pl.ds((1, 0, 3, 2)[f], 1)]
+                        level = jnp.where(holder == float(r), edge, level)
+                    ghost[3, row] = jnp.where(linked, level, own[3, row])
+                for q in range(3):
                     mine = own[q, row]
                     if q == (1 if f < 2 else 2):
                         mine = -mine
@@ -355,21 +389,71 @@
             columns[t, rows] = edge_columns(t, rows, 2, v, value)
         return carry
 
+    def send_terrain():
+        def send_edges(to_band, to_peer):
+            pltpu.make_async_remote_copy(
+                src_ref=edge_msgs.at[to_band],
+                dst_ref=edge_in.at[me],
+                send_sem=terrain_send.at[2],
+                recv_sem=terrain_recv.at[2],
+                device_id=place(to_band, to_peer),
+                device_id_type=MESH,
+            ).start()
+
+        each_other(send_edges)
+        for part, (source, target) in enumerate(((out_bed, in_bed), (out_rough, in_rough))):
+            for offset in range(1, bands):
+                to_band = lax.rem(band + offset, bands)
+                pltpu.make_async_remote_copy(
+                    src_ref=source.at[to_band],
+                    dst_ref=target.at[band],
+                    send_sem=terrain_send.at[part],
+                    recv_sem=terrain_recv.at[part],
+                    device_id=place(to_band, peer),
+                    device_id_type=MESH,
+                ).start()
+
+    def fill_bed():
+        wait_for(in_bed, bands - 1, terrain_recv.at[0])
+        for t in range(slots):
+            fetched = in_bed[jnp.maximum(source_ref[t], 0)].astype(jnp.float32)
+            level = jnp.where(source_ref[t] >= 0, fetched, local_ref[0, t].astype(jnp.float32))
+            bed[t, pl.ds(0, size)] = level
+            prim[0, t, pl.ds(0, size)] = level + state_ref[0, t]
+            own[3, pl.ds(2 * slots + t, 1)] = level[0:1]
+            own[3, pl.ds(3 * slots + t, 1)] = level[size - 1 : size]
+
+    def own_edges():
+        wait_for(edge_in, total - 1, terrain_recv.at[2])
+        for t in range(slots):
+            holder = jnp.maximum(source_ref[t], 0) * peers + peer
+            for f in range(2):
+                row = pl.ds(f * slots + t, 1)
+                edge = edge_in[holder, pl.ds(f, 1)]
+                own[3, row] = jnp.where(source_ref[t] >= 0, edge, own[3, row])
+
+    def fill_drag():
+        wait_for(in_rough, bands - 1, terrain_recv.at[1])
+        for t in range(slots):
+            fetched = in_rough[jnp.maximum(source_ref[t], 0)].astype(jnp.float32)
+            rough = jnp.where(source_ref[t] >= 0, fetched, local_ref[1, t].astype(jnp.float32))
+            drag[t] = (DT * GRAVITY) * rough * rough
+
     for step in range(STEPS):
         send_strips(step)
+        if step == 0:
+            send_terrain()
+            fill_bed()
         lax.fori_loop(0, slots * chunks, inner, 0)
+        wait_strips(step)
         if step == 0:
-            wait_for(in_rough, bands - 1, terrain_recv.at[1])
-            for t in range(slots):
-                fetched = in_rough[jnp.maximum(source_ref[t], 0)].astype(jnp.float32)
-                rough = jnp.where(
-                    source_ref[t] >= 0, fetched, local_ref[1, t].astype(jnp.float32)
-                )
-                drag[t] = (DT * GRAVITY) * rough * rough
-        wait_strips(step)
+            own_edges()
         rims(step)
+        if step == 0:
+            fill_drag()
         lax.fori_loop(0, slots * chunks, functools.partial(update, step), 0)
 
+    wait_for(edge_in, total - 1, terrain_send.at[2])
     for part, source in enumerate((out_bed, out_rough)):
         wait_for(source, bands - 1, terrain_send.at[part])
     for step in range(STEPS):
@@ -389,15 +473,22 @@
     peers = subs * lanes
     f32, bf16 = jnp.float32, jnp.bfloat16
     block = (bands, size, size)
-    smem = pl.BlockSpec(memory_space=pltpu.SMEM)
+    hbm = pl.BlockSpec(memory_space=pl.ANY)
     vmem = pl.BlockSpec(memory_space=pltpu.VMEM)
     msg = (4 * slots, size)
     return pl.pallas_call(
         functools.partial(kernel, sizes),
         out_shape=jax.ShapeDtypeStruct(state.shape, f32),
-        in_specs=[smem] * 4 + [vmem] * 3,
+        in_specs=[hbm] * 7,
         out_specs=vmem,
         scratch_shapes=[
+            pltpu.SMEM(wet_count.shape, jnp.int32),
+            pltpu.SMEM(face_links.shape, jnp.int32),
+            pltpu.SMEM(new_source.shape, jnp.int32),
+            pltpu.SMEM(store_target.shape, jnp.int32),
+            pltpu.VMEM(state.shape, f32),
+            pltpu.VMEM(terrain_local.shape, bf16),
+            pltpu.VMEM(terrain_store.shape, bf16),
             pltpu.VMEM(block, bf16),
             pltpu.VMEM(block, bf16),
             pltpu.VMEM(block, bf16),
@@ -417,8 +508,11 @@
             [pltpu.VMEM((peers, 2) + msg, f32) for _ in range(STEPS)],
             [pltpu.VMEM((peers,) + msg, f32) for _ in range(STEPS)],
             [pltpu.VMEM((peers,) + msg, f32) for _ in range(STEPS)],
-            pltpu.SemaphoreType.DMA((2,)),
-            pltpu.SemaphoreType.DMA((2,)),
+            pltpu.VMEM((bands, 8, size), f32),
+            pltpu.VMEM((bands * peers, 8, size), f32),
+            pltpu.SemaphoreType.DMA((7,)),
+            pltpu.SemaphoreType.DMA((3,)),
+            pltpu.SemaphoreType.DMA((3,)),
             pltpu.SemaphoreType.DMA((STEPS, 3)),
             pltpu.SemaphoreType.DMA((STEPS, 3)),
         ],

time: 32 us -> 28.8 us (0.900)
  Pallas kernels: 26.8 us -> 23.6 us
    pallas_call x1, Pallas kernels: 26.8 us -> 23.6 us  [local(): pl.pallas_call(functools.partial(kernel, sizes), out_shape=jax.ShapeDtype...]
where the time goes in v2:
time: 28.8 us; the launch traced here: 28.6 us
  Pallas kernels  23.6 us (82%)
  local copies, waits for them, and re-layouts  4.28 us (15%)
  between operations  0.72 us (2%)
    pallas_call x1, Pallas kernels, local(): pl.pallas_call(functools.partial(kernel, sizes), out_shape=jax.ShapeDtype...  23.6 us
    unnamed x13, local copies, waits for them, and re-layouts  4.28 us

profile of v2, /device:TPU:0, one launch (start us, length us, event | category | flops | bytes accessed | tf_op | source)
XLA Modules:
  0.0 28.6 jit_solution(13978462016178089115)
XLA Ops:
  0.0 0.0 copy-start.5
  0.0 0.0 copy-start.4
  0.7 0.0 copy-done.5
  0.7 0.0 copy-done.4
  0.7 0.0 copy-start
  0.7 1.0 %copy-done = f32[3,2,128,128]{3,2,1,0:T(8,128)S(1)} copy-done((f32[3,2,128,128]{3,2,1,0:T(8,128)S(1)}, f32[3,2,128,128]{3,2,1,0:T(8,128)}, u32[]{:S(2)}) %copy-start) | copy-done | bytes 393240
  1.7 0.0 copy-start.1
  1.7 0.9 %copy-done.1 = bf16[2,4,128,128]{3,2,1,0:T(8,128)(2,1)S(1)} copy-done((bf16[2,4,128,128]{3,2,1,0:T(8,128)(2,1)S(1)}, bf16[2,4,128,128]{3,2,1,0:T(8,128)(2,1)}, u32[]{:S(2)}) %copy-start.1) | copy-done | bytes 262168
  2.7 0.0 copy-start.2
  2.7 0.9 %copy-done.2 = bf16[2,2,128,128]{3,2,1,0:T(8,128)(2,1)S(1)} copy-done((bf16[2,2,128,128]{3,2,1,0:T(8,128)(2,1)S(1)}, bf16[2,2,128,128]{3,2,1,0:T(8,128)(2,1)}, u32[]{:S(2)}) %copy-start.2) | copy-done | bytes 131096
  3.6 0.0 copy-start.3
  3.6 0.7 %copy-done.3 = s32[2,2,4]{2,1,0:T(2,128)S(1)} copy-done((s32[2,2,4]{2,1,0:T(2,128)S(1)}, s32[2,2,4]{2,1,0:T(2,128)}, u32[]{:S(2)}) %copy-start.3) | copy-done | bytes 88
  4.2 23.6 %shard_map.73 = f32[3,2,128,128]{3,2,1,0:T(8,128)S(1)} custom-call(s32[1]{0:T(128)S(6)} %copy.9.wet_hbm, s32[2,2,4]{2,1,0:T(2,128)S(1)} %copy-done.3, s32[2]{0:T(128)S(1)} %copy-done.4, s32[4]{0:T(128)S(1)} %copy-done.5, f32[3,2,128,128]{3,2,1,0:T(8,128)S(1)} %copy-done, bf16[2,2,128,128]{3,2,1,0:T(8,128)(2,1)S(1)} %copy-done.2, ...), custom_call_target="tpu_custom_call" | custom-call | tf_op jit(solution)/shard_map/pallas_call | solution.py:479
  27.8 0.7 %copy.10 = f32[3,2,128,128]{3,2,1,0:T(8,128)} copy(f32[3,2,128,128]{3,2,1,0:T(8,128)S(1)} %shard_map.73) | data formatting | bytes 786432
Async XLA Ops:
  0.0 0.7 %copy-start.5 = (s32[4]{0:T(128)S(1)}, s32[4]{0:T(128)}, u32[]{:S(2)}) copy-start(s32[4]{0:T(128)} %target_hbm.1) | copy-start | bytes 52
  0.0 0.7 %copy-start.4 = (s32[2]{0:T(128)S(1)}, s32[2]{0:T(128)}, u32[]{:S(2)}) copy-start(s32[2]{0:T(128)} %source_hbm.1) | copy-start | bytes 28
  0.7 1.0 %copy-start = (f32[3,2,128,128]{3,2,1,0:T(8,128)S(1)}, f32[3,2,128,128]{3,2,1,0:T(8,128)}, u32[]{:S(2)}) copy-start(f32[3,2,128,128]{3,2,1,0:T(8,128)} %state_hbm.1) | copy-start | bytes 1179652
  1.7 0.9 %copy-start.1 = (bf16[2,4,128,128]{3,2,1,0:T(8,128)(2,1)S(1)}, bf16[2,4,128,128]{3,2,1,0:T(8,128)(2,1)}, u32[]{:S(2)}) copy-start(bf16[2,4,128,128]{3,2,1,0:T(8,128)(2,1)} %store_hbm.1) | copy-start | bytes 786436
  2.7 0.9 %copy-start.2 = (bf16[2,2,128,128]{3,2,1,0:T(8,128)(2,1)S(1)}, bf16[2,2,128,128]{3,2,1,0:T(8,128)(2,1)}, u32[]{:S(2)}) copy-start(bf16[2,2,128,128]{3,2,1,0:T(8,128)(2,1)} %local_hbm.1) | copy-start | bytes 393220
  3.6 0.7 %copy-start.3 = (s32[2,2,4]{2,1,0:T(2,128)S(1)}, s32[2,2,4]{2,1,0:T(2,128)}, u32[]{:S(2)}) copy-start(s32[2,2,4]{2,1,0:T(2,128)} %links_hbm.1) | copy-start | bytes 196

commit v3 on v2

--- a/solution.py
+++ b/solution.py
@@ -12,6 +12,7 @@
 CELL = 30.0
 DT = 1.0
 ROWS = 128
+CODE = 4096.0
 AXES = ("region", "tile", "sub", "lane")
 MESH = pl.DeviceIdType.MESH
 
@@ -163,9 +164,6 @@
     for r in range(bands):
         edge_msgs[r, pl.ds(0, 1)] = sides[2 * r + 1 : 2 * r + 2]
         edge_msgs[r, pl.ds(1, 1)] = sides[2 * r : 2 * r + 1]
-        for t in range(slots):
-            row = jnp.full((1, size), source_ref[t].astype(jnp.float32))
-            edge_msgs[r, pl.ds(4 + t, 1)] = row
     in_bed[band] = out_bed[band]
     in_rough[band] = out_rough[band]
     edge_in[me] = edge_msgs[band]
@@ -213,8 +211,12 @@
                     top, low = prim[q, t, pl.ds(0, 1)], prim[q, t, pl.ds(size - 1, 1)]
                 strip = (turned[2 * q + 1 : 2 * q + 2], turned[2 * q : 2 * q + 1], top, low)
                 for f in range(4):
-                    msgs[step, f, pl.ds(4 * t + q, 1)] = strip[f]
                     own[q, pl.ds(f * slots + t, 1)] = strip[f]
+                    sent = strip[f]
+                    if q == 3:
+                        code = CODE * (source_ref[t].astype(jnp.float32) + 1.0)
+                        sent = jnp.where(source_ref[t] >= 0, code, sent)
+                    msgs[step, f, pl.ds(4 * t + q, 1)] = sent
         strips_x[step][peer] = msgs[step, pl.ds(0, 2)]
         if step == 0:
             pl.semaphore_wait(barrier, total - 1)
@@ -297,12 +299,11 @@
                     remote = (strips_n if f == 2 else strips_s)[step][who, rows]
                 row = pl.ds(f * slots + t, 1)
                 if step == 0:
-                    at = band + (0, 0, -1, 1)[f]
-                    holder = edge_in[jnp.clip(at, 0, bands - 1) * peers + who, pl.ds(4 + slot, 1)]
-                    level = remote[3:4]
+                    told = remote[3:4]
+                    level = told
                     for r in range(bands):
                         edge = edge_in[r * peers + who, pl.ds((1, 0, 3, 2)[f], 1)]
-                        level = jnp.where(holder == float(r), edge, level)
+                        level = jnp.where(told == CODE * (r + 1.0), edge, level)
                     ghost[3, row] = jnp.where(linked, level, own[3, row])
                 for q in range(3):
                     mine = own[q, row]
@@ -454,8 +455,8 @@
         lax.fori_loop(0, slots * chunks, functools.partial(update, step), 0)
 
     wait_for(edge_in, total - 1, terrain_send.at[2])
-    for part, source in enumerate((out_bed, out_rough)):
-        wait_for(source, bands - 1, terrain_send.at[part])
+    wait_for(out_rough, bands - 1, terrain_send.at[1])
+    wait_for(out_bed, bands - 1, terrain_send.at[0])
     for step in range(STEPS):
         wait_for(strips_x[step], peers - 1, strip_send.at[step, 0])
 
@@ -473,7 +474,7 @@
     peers = subs * lanes
     f32, bf16 = jnp.float32, jnp.bfloat16
     block = (bands, size, size)
-    hbm = pl.BlockSpec(memory_space=pl.ANY)
+    hbm = pl.BlockSpec(memory_space=pltpu.HBM)
     vmem = pl.BlockSpec(memory_space=pltpu.VMEM)
     msg = (4 * slots, size)
     return pl.pallas_call(
@@ -508,8 +509,8 @@
             [pltpu.VMEM((peers, 2) + msg, f32) for _ in range(STEPS)],
             [pltpu.VMEM((peers,) + msg, f32) for _ in range(STEPS)],
             [pltpu.VMEM((peers,) + msg, f32) for _ in range(STEPS)],
-            pltpu.VMEM((bands, 8, size), f32),
-            pltpu.VMEM((bands * peers, 8, size), f32),
+            pltpu.VMEM((bands, 4, size), f32),
+            pltpu.VMEM((bands * peers, 4, size), f32),
             pltpu.SemaphoreType.DMA((7,)),
             pltpu.SemaphoreType.DMA((3,)),
             pltpu.SemaphoreType.DMA((3,)),
@@ -517,7 +518,7 @@
             pltpu.SemaphoreType.DMA((STEPS, 3)),
         ],
         compiler_params=pltpu.CompilerParams(
-            collective_id=0, has_side_effects=True, vmem_limit_bytes=32 * 1024 * 1024
+            collective_id=0, has_side_effects=True, vmem_limit_bytes=64 * 1024 * 1024
         ),
     )(wet_count, face_links, new_source, store_target, state, terrain_local, terrain_store)
 

time: 28.8 us -> 25.9 us (0.90)
  local copies, waits for them, and re-layouts: 4.28 us -> 1.77 us
  Pallas kernels: 23.6 us -> 23.3 us
    unnamed x13 -> x1, local copies, waits for them, and re-layouts: 4.28 us -> 1.77 us
    pallas_call x1, Pallas kernels: 23.6 us -> 23.3 us  [local(): pl.pallas_call(functools.partial(kernel, sizes), out_shape=jax.ShapeDtype...]
where the time goes in v3:
time: 25.9 us; the launch traced here: 25.7 us
  Pallas kernels  23.3 us (90%)
  local copies, waits for them, and re-layouts  1.77 us (7%)
  between operations  0.66 us (3%)
    pallas_call x1, Pallas kernels, local(): pl.pallas_call(functools.partial(kernel, sizes), out_shape=jax.ShapeDtype...  23.3 us
    unnamed x1, local copies, waits for them, and re-layouts  1.77 us

profile of v3, /device:TPU:0, one launch (start us, length us, event | category | flops | bytes accessed | tf_op | source)
XLA Modules:
  0.0 25.7 jit_solution(1985700184915390594)
XLA Ops:
  0.7 23.3 %shard_map.73 = f32[3,2,128,128]{3,2,1,0:T(8,128)} custom-call(s32[1]{0:T(128)S(6)} %copy.9.wet_hbm, s32[2,2,4]{2,1,0:T(2,128)} %links_hbm.1, s32[2]{0:T(128)} %source_hbm.1, s32[4]{0:T(128)} %target_hbm.1, f32[3,2,128,128]{3,2,1,0:T(8,128)} %state_hbm.1, bf16[2,2,128,128]{3,2,1,0:T(8,128)(2,1)} %local_hbm.1, bf16[2,4,128,128]{3,2,1,0:T(8,128)(2,1)} %store_hbm.1), custom_call_target="tpu_custom_call" | custom-call | tf_op jit(solution)/shard_map/pallas_call | solution.py:480
  23.9 1.8 %copy.10 = f32[3,2,128,128]{3,2,1,0:T(8,128)} copy(f32[3,2,128,128]{3,2,1,0:T(8,128)} %shard_map.73) | data formatting | bytes 786432

commit v4 on v3

--- a/solution.py
+++ b/solution.py
@@ -479,7 +479,7 @@
     msg = (4 * slots, size)
     return pl.pallas_call(
         functools.partial(kernel, sizes),
-        out_shape=jax.ShapeDtypeStruct(state.shape, f32),
+        out_shape=pltpu.VMEM(state.shape, f32),
         in_specs=[hbm] * 7,
         out_specs=vmem,
         scratch_shapes=[
@@ -518,7 +518,7 @@
             pltpu.SemaphoreType.DMA((STEPS, 3)),
         ],
         compiler_params=pltpu.CompilerParams(
-            collective_id=0, has_side_effects=True, vmem_limit_bytes=64 * 1024 * 1024
+            collective_id=0, has_side_effects=True, vmem_limit_bytes=63 * 1024 * 1024
         ),
     )(wet_count, face_links, new_source, store_target, state, terrain_local, terrain_store)
 

time: 25.9 us -> 24.1 us (0.931)
  local copies, waits for them, and re-layouts: 1.77 us -> 0.75 us
  Pallas kernels: 23.3 us -> 22.5 us
    unnamed x1, local copies, waits for them, and re-layouts: 1.77 us -> 0.75 us
    pallas_call x1, Pallas kernels: 23.3 us -> 22.5 us  [local(): pl.pallas_call(functools.partial(kernel, sizes), out_shape=pltpu.VMEM(sta...]
where the time goes in v4:
time: 24.1 us; the launch traced here: 23.9 us
  Pallas kernels  22.5 us (93%)
  local copies, waits for them, and re-layouts  0.75 us (3%)
  between operations  0.66 us (3%)
    pallas_call x1, Pallas kernels, local(): pl.pallas_call(functools.partial(kernel, sizes), out_shape=pltpu.VMEM(sta...  22.5 us
    unnamed x1, local copies, waits for them, and re-layouts  0.75 us

profile of v4, /device:TPU:0, one launch (start us, length us, event | category | flops | bytes accessed | tf_op | source)
XLA Modules:
  0.0 23.9 jit_solution(8034027920244275004)
XLA Ops:
  0.7 22.5 %shard_map.73 = f32[3,2,128,128]{3,2,1,0:T(8,128)S(1)} custom-call(s32[1]{0:T(128)S(6)} %copy.10.wet_hbm, s32[2,2,4]{2,1,0:T(2,128)} %links_hbm.1, s32[2]{0:T(128)} %source_hbm.1, s32[4]{0:T(128)} %target_hbm.1, f32[3,2,128,128]{3,2,1,0:T(8,128)} %state_hbm.1, bf16[2,2,128,128]{3,2,1,0:T(8,128)(2,1)} %local_hbm.1, bf16[2,4,128,128]{3,2,1,0:T(8,128)(2,1)} %store_hbm.1), custom_call_target="tpu_custom_call" | custom-call | tf_op jit(solution)/shard_map/pallas_call | solution.py:480
  23.2 0.7 %copy.9 = f32[3,2,128,128]{3,2,1,0:T(8,128)} copy(f32[3,2,128,128]{3,2,1,0:T(8,128)S(1)} %shard_map.73) | data formatting | bytes 786432

commit v5 on v4

--- a/solution.py
+++ b/solution.py
@@ -445,14 +445,14 @@
         if step == 0:
             send_terrain()
             fill_bed()
-        lax.fori_loop(0, slots * chunks, inner, 0)
+        lax.fori_loop(0, slots * chunks, inner, 0, unroll=True)
         wait_strips(step)
         if step == 0:
             own_edges()
         rims(step)
         if step == 0:
             fill_drag()
-        lax.fori_loop(0, slots * chunks, functools.partial(update, step), 0)
+        lax.fori_loop(0, slots * chunks, functools.partial(update, step), 0, unroll=True)
 
     wait_for(edge_in, total - 1, terrain_send.at[2])
     wait_for(out_rough, bands - 1, terrain_send.at[1])

time: 24.1 us -> 23.7 us (0.983)
  Pallas kernels: 22.5 us -> 22.1 us
    pallas_call x1, Pallas kernels: 22.5 us -> 22.1 us  [local(): pl.pallas_call(functools.partial(kernel, sizes), out_shape=pltpu.VMEM(sta...]
where the time goes in v5:
time: 23.7 us; the launch traced here: 23.5 us
  Pallas kernels  22.1 us (93%)
  local copies, waits for them, and re-layouts  0.75 us (3%)
  between operations  0.66 us (3%)
    pallas_call x1, Pallas kernels, local(): pl.pallas_call(functools.partial(kernel, sizes), out_shape=pltpu.VMEM(sta...  22.1 us
    unnamed x1, local copies, waits for them, and re-layouts  0.75 us

profile of v5, /device:TPU:0, one launch (start us, length us, event | category | flops | bytes accessed | tf_op | source)
XLA Modules:
  0.0 23.5 jit_solution(13217966523776111930)
XLA Ops:
  0.7 22.1 %shard_map.73 = f32[3,2,128,128]{3,2,1,0:T(8,128)S(1)} custom-call(s32[1]{0:T(128)S(6)} %copy.10.wet_hbm, s32[2,2,4]{2,1,0:T(2,128)} %links_hbm.1, s32[2]{0:T(128)} %source_hbm.1, s32[4]{0:T(128)} %target_hbm.1, f32[3,2,128,128]{3,2,1,0:T(8,128)} %state_hbm.1, bf16[2,2,128,128]{3,2,1,0:T(8,128)(2,1)} %local_hbm.1, bf16[2,4,128,128]{3,2,1,0:T(8,128)(2,1)} %store_hbm.1), custom_call_target="tpu_custom_call" | custom-call | tf_op jit(solution)/shard_map/pallas_call | solution.py:480
  22.7 0.7 %copy.9 = f32[3,2,128,128]{3,2,1,0:T(8,128)} copy(f32[3,2,128,128]{3,2,1,0:T(8,128)S(1)} %shard_map.73) | data formatting | bytes 786432
